TPU v7x, 128 devices: a whole 4x4x4 slice. The times are simulated.
128 devices in a mesh: gz: 8 (over x, core), xy: 16 (over y, z).
Axes of the slice: x: 4, y: 4, z: 4, core: 2. Of those that a mesh axis runs over, the one named last changes fastest.
Arguments:
- patches: bfloat16 [2048, 128, 256], P(('gz', 'xy'))
- pair_leaves: int32 [24576, 2], P(('gz', 'xy')), may hold values from 0 to 2047, as said below
- pair_count: int32 [128], replicated, may hold values from 1 to 192, as said below
Outputs:
- denoised: bfloat16 [2048, 128, 256], P(('gz', 'xy'))
Inputs may be any that keep to these rules, and one draw needn't show every extreme that they name: `pair_leaves`: row r belongs to device r // 192. Column 0 is a leaf held by that device; column 1 is a larger leaf id held by that device or one of the next two. Rows at or past that device's pair_count are ignored. `pair_count`: some device has exactly 192 live pairs.
All inputs are finite; a program needn't handle non-finite values.
Results may differ from a plain program's by a relative error of at most 0.005.
Values may be sent and summed in bfloat16 or wider, within the bound.
A program may use at most 64 MiB of HBM per device.

v0:
```python
import jax
import jax.numpy as jnp
from jax import lax
from jax.sharding import PartitionSpec as P

GROUP = 8
ROUNDS = 2


def passed_along(block, axis, distance):
    devices = range(lax.axis_size(axis))
    route = [(i - distance, i) for i in devices if i - distance in devices]
    return lax.ppermute(block, axis, route)


def accumulate(window, lookup, load, anchor, spread):
    slots_here = window.shape[0]
    leaf_rows = window.shape[1]
    width = window.shape[2]
    top_row = slots_here - 1

    def advance(turn_index, carry):
        numerator, denominator = carry
        places = turn_index * GROUP + jnp.arange(GROUP, dtype=jnp.int32)
        records = lookup(places)
        alive = (places < load).astype(jnp.float32)
        left_rows = jnp.clip(records[:, 0] - anchor, 0, top_row)
        right_rows = jnp.clip(records[:, 1] - anchor, 0, top_row)
        both_rows = jnp.concatenate([left_rows, right_rows])
        picked = jnp.take(window, both_rows, axis=0)
        left_patch = picked[:GROUP]
        right_patch = picked[GROUP:]
        powers = jnp.sum(jnp.square(picked.astype(jnp.float32)), axis=2)
        crossed = jnp.einsum(
            "gik,gjk->gij", left_patch, right_patch, preferred_element_type=jnp.float32
        )
        distance = powers[:GROUP][:, :, None] + powers[GROUP:][:, None, :] - 2.0 * crossed
        weights = jnp.exp(-distance / spread) * alive[:, None, None]
        rounded = weights.astype(jnp.bfloat16)
        to_left = jnp.einsum(
            "gij,gjk->gik", rounded, right_patch, preferred_element_type=jnp.float32
        )
        to_right = jnp.einsum(
            "gij,gik->gjk", rounded, left_patch, preferred_element_type=jnp.float32
        )
        terms = jnp.concatenate([to_left, to_right], axis=0)
        sums = jnp.concatenate([jnp.sum(weights, axis=2), jnp.sum(weights, axis=1)], axis=0)
        numerator = numerator.at[both_rows].add(terms)
        denominator = denominator.at[both_rows].add(sums)
        return (numerator, denominator)

    turns = (load + GROUP - 1) // GROUP
    start = (
        jnp.zeros((slots_here, leaf_rows, width), jnp.float32),
        jnp.zeros((slots_here, leaf_rows), jnp.float32),
    )
    numerator, denominator = lax.fori_loop(0, turns, advance, start)
    return (numerator, denominator)


def denoise(current, lookup, load, anchor):
    leaves = current.shape[0]
    spread = current.shape[2] / 4.0
    before = jnp.zeros_like(current)
    ahead_blocks = [passed_along(current, ("gz", "xy"), -step) for step in (1, 2)]
    window = jnp.concatenate([before, current, ahead_blocks[0], ahead_blocks[1]], axis=0)
    numerator, denominator = accumulate(window, lookup, load, anchor, spread)
    pieces = [
        (
            numerator[slot * leaves : (slot + 1) * leaves],
            denominator[slot * leaves : (slot + 1) * leaves],
        )
        for slot in range(4)
    ]
    own_numer, own_denom = pieces[1]
    for step in (1, 2):
        arrived = passed_along((pieces[1 + step][0], pieces[1 + step][1]), ("gz", "xy"), step)
        own_numer = own_numer + arrived[0]
        own_denom = own_denom + arrived[1]
    total = (current.astype(jnp.float32) + own_numer) / (1.0 + own_denom)[:, :, None]
    return total.astype(jnp.bfloat16)


def on_device(patches, pair_leaves, pair_count):
    device_id = lax.axis_index(("gz", "xy"))
    leaves = patches.shape[0]
    slots = pair_leaves.shape[0]
    anchor = (device_id - 1) * leaves
    mine = pair_count[device_id]

    def lookup(places):
        return pair_leaves[jnp.minimum(places, slots - 1)]

    current = patches
    for round_index in range(ROUNDS):
        current = denoise(current, lookup, mine, anchor)
    return current


def solution(mesh):
    return jax.shard_map(
        on_device,
        mesh=mesh,
        in_specs=(P(("gz", "xy"), None, None), P(("gz", "xy"), None), P()),
        out_specs=P(("gz", "xy"), None, None),
        check_vma=False,
    )
```

profile of v0, /device:TPU:17, one launch (start us, length us, event | category | flops | bytes accessed | tf_op | source)
XLA Modules:
  0.0 890.4 jit_solution(14509994735613309717)
XLA Ops:
  0.0 5.5 collective-permute-start
  5.6 1.9 collective-permute-start.1
  10.2 39.4 %collective-permute-done = bf16[16,128,256]{2,1,0:T(8,128)(2,1)S(1)} collective-permute-done((bf16[16,128,256]{2,1,0:T(8,128)(2,1)}, bf16[16,128,256]{2,1,0:T(8,128)(2,1)S(1)}, u32[]{:S(2)}, u32[]{:S(2)}) %collective-permute-start) | collective-permute-done | bytes 1048608 | tf_op jit(solution)/shard_map/ppermute | solution.py:13
  49.7 22.6 %collective-permute-done.1 = bf16[16,128,256]{2,1,0:T(8,128)(2,1)S(1)} collective-permute-done((bf16[16,128,256]{2,1,0:T(8,128)(2,1)}, bf16[16,128,256]{2,1,0:T(8,128)(2,1)S(1)}, u32[]{:S(2)}, u32[]{:S(2)}) %collective-permute-start.1) | collective-permute-done | bytes 1048608 | tf_op jit(solution)/shard_map/ppermute | solution.py:13
  72.2 3.3 pad_maximum_fusion.2
  75.5 4.2 broadcast.202.clone
  79.8 104.3 %while.24 = (s32[]{:T(128)}, f32[64,128,256]{2,1,0:T(8,128)}, f32[64,128]{1,0:T(8,128)S(1)}, s32[]{:T(128)}, s32[192,2]{1,0:T(8,128)S(1)}, /*index=5*/s32[]{:T(1...) while((s32[]{:T(128)}, f32[64,128,256]{2,1,0:T(8,128)}, ...), condition=%wide.region_6.8_spmd, body=%wide.region_0.7_spmd.sunk | while | flops 205654288 | bytes 20276908 | solution.py:57
  81.6 2.8 gather_fusion.1
  86.9 4.4 scatter_fusion
  93.1 2.8 gather_fusion.1
  98.4 4.5 scatter_fusion
  104.7 2.8 gather_fusion.1
  110.0 4.5 scatter_fusion
  116.3 2.8 gather_fusion.1
  121.6 4.5 scatter_fusion
  127.9 2.8 gather_fusion.1
  133.2 4.4 scatter_fusion
  139.4 2.8 gather_fusion.1
  144.7 4.4 scatter_fusion
  151.0 2.8 gather_fusion.1
  156.2 4.5 scatter_fusion
  162.6 2.8 gather_fusion.1
  167.8 4.5 scatter_fusion
  174.2 2.8 gather_fusion.1
  179.5 4.5 scatter_fusion
  184.0 2.6 fusion.45
  186.6 27.8 %collective-permute-start.2 = (f32[16,128,256]{2,1,0:T(8,128)S(1)}, f32[16,128,256]{2,1,0:T(8,128)S(1)}, u32[]{:S(2)}, u32[]{:S(2)}) collective-permute-start(f32[16,128,256]{2,1,0:T(8,128)S(1)} %get-tuple-element.210), channel_id=1, source_target_pairs={{0,1},{1,2},{2,3},{3,4},{4,5},{5,6},{6,7},{7,8},{8,9},{9,10},{10,1... | collective-permute-start | bytes 6291464 | tf_op jit(solution)/shard_map/ppermute | solution.py:13
  214.4 1.9 collective-permute-start.3
  216.3 1.9 collective-permute-start.4
  218.3 17.6 %collective-permute-start.5 = (f32[16,128]{1,0:T(8,128)S(1)}, f32[16,128]{1,0:T(8,128)S(1)}, u32[]{:S(2)}, u32[]{:S(2)}) collective-permute-start(f32[16,128]{1,0:T(8,128)S(1)} %get-tuple-element.215), channel_id=1, source_target_pairs={{0,2},{1,3},{2,4},{3,5},{4,6},{5,7},{6,8},{7,9},{8,10},{9,11},{10,... | collective-permute-start | bytes 24584 | tf_op jit(solution)/shard_map/ppermute | solution.py:13
  235.9 232.3 %collective-permute-done.4 = f32[16,128]{1,0:T(8,128)S(1)} collective-permute-done((f32[16,128]{1,0:T(8,128)S(1)}, f32[16,128]{1,0:T(8,128)S(1)}, u32[]{:S(2)}, u32[]{:S(2)}) %collective-permute-start.4) | collective-permute-done | bytes 8224 | tf_op jit(solution)/shard_map/ppermute | solution.py:13
  468.2 2.2 divide_convert_fusion.1
  470.4 1.9 collective-permute-start.7
  472.3 1.9 collective-permute-start.6
  474.3 21.9 %collective-permute-done.7 = bf16[16,128,256]{2,1,0:T(8,128)(2,1)S(1)} collective-permute-done((bf16[16,128,256]{2,1,0:T(8,128)(2,1)S(1)}, bf16[16,128,256]{2,1,0:T(8,128)(2,1)S(1)}, u32[]{:S(2)}, u32[]{:S(2)}) %collective-permute-start.7) | collective-permute-done | bytes 1048608 | tf_op jit(solution)/shard_map/ppermute | solution.py:13
  496.2 16.3 %collective-permute-done.6 = bf16[16,128,256]{2,1,0:T(8,128)(2,1)S(1)} collective-permute-done((bf16[16,128,256]{2,1,0:T(8,128)(2,1)S(1)}, bf16[16,128,256]{2,1,0:T(8,128)(2,1)S(1)}, u32[]{:S(2)}, u32[]{:S(2)}) %collective-permute-start.6) | collective-permute-done | bytes 1048608 | tf_op jit(solution)/shard_map/ppermute | solution.py:13
  512.4 3.7 pad_maximum_fusion.3
  516.1 4.2 broadcast.202
  520.4 104.2 %while.25 = (s32[]{:T(128)}, f32[64,128,256]{2,1,0:T(8,128)}, f32[64,128]{1,0:T(8,128)S(1)}, s32[]{:T(128)}, s32[192,2]{1,0:T(8,128)S(1)}, /*index=5*/s32[]{:T(1...) while((s32[]{:T(128)}, f32[64,128,256]{2,1,0:T(8,128)}, ...), condition=%wide.region_13.15_spmd, body=%wide.region_7.14_spmd.sunk | while | flops 205654288 | bytes 20276908 | solution.py:57
  522.2 2.8 gather_fusion.3
  527.5 4.4 scatter_fusion.1
  533.7 2.8 gather_fusion.3
  539.0 4.5 scatter_fusion.1
  545.3 2.8 gather_fusion.3
  550.5 4.5 scatter_fusion.1
  556.9 2.8 gather_fusion.3
  562.2 4.5 scatter_fusion.1
  568.5 2.8 gather_fusion.3
  573.7 4.4 scatter_fusion.1
  580.0 2.8 gather_fusion.3
  585.3 4.4 scatter_fusion.1
  591.5 2.8 gather_fusion.3
  596.8 4.5 scatter_fusion.1
  603.1 2.8 gather_fusion.3
  608.4 4.5 scatter_fusion.1
  614.8 2.8 gather_fusion.3
  620.1 4.5 scatter_fusion.1
  624.6 2.5 fusion.44
  627.1 52.2 %collective-permute-start.8 = (f32[16,128,256]{2,1,0:T(8,128)S(1)}, f32[16,128,256]{2,1,0:T(8,128)S(1)}, u32[]{:S(2)}, u32[]{:S(2)}) collective-permute-start(f32[16,128,256]{2,1,0:T(8,128)S(1)} %get-tuple-element.208), channel_id=1, source_target_pairs={{0,1},{1,2},{2,3},{3,4},{4,5},{5,6},{6,7},{7,8},{8,9},{9,10},{10,1... | collective-permute-start | bytes 6291464 | tf_op jit(solution)/shard_map/ppermute | solution.py:13
  679.4 1.9 collective-permute-start.9
  681.3 1.9 collective-permute-start.10
  683.2 1.9 collective-permute-start.11
  685.2 202.0 %collective-permute-done.10 = f32[16,128]{1,0:T(8,128)S(1)} collective-permute-done((f32[16,128]{1,0:T(8,128)S(1)}, f32[16,128]{1,0:T(8,128)S(1)}, u32[]{:S(2)}, u32[]{:S(2)}) %collective-permute-start.10) | collective-permute-done | bytes 8224 | tf_op jit(solution)/shard_map/ppermute | solution.py:13
  887.2 3.2 divide_convert_fusion
  (324 shorter events, 78.2 us)
Async XLA Ops:
  0.0 49.7 %collective-permute-start = (bf16[16,128,256]{2,1,0:T(8,128)(2,1)}, bf16[16,128,256]{2,1,0:T(8,128)(2,1)S(1)}, u32[]{:S(2)}, u32[]{:S(2)}) collective-permute-start(bf16[16,128,256]{2,1,0:T(8,128)(2,1)} %param.9), channel_id=1, source_target_pairs={{1,0},{2,1},{3,2},{4,3},{5,4},{6,5},{7,6},{8,7},{9,8},{10,9},{11,1... | collective-permute-start | bytes 3145736 | tf_op jit(solution)/shard_map/ppermute | solution.py:13
  5.6 66.7 %collective-permute-start.1 = (bf16[16,128,256]{2,1,0:T(8,128)(2,1)}, bf16[16,128,256]{2,1,0:T(8,128)(2,1)S(1)}, u32[]{:S(2)}, u32[]{:S(2)}) collective-permute-start(bf16[16,128,256]{2,1,0:T(8,128)(2,1)} %param.9), channel_id=1, source_target_pairs={{2,0},{3,1},{4,2},{5,3},{6,4},{7,5},{8,6},{9,7},{10,8},{11,9},{12,... | collective-permute-start | bytes 3145736 | tf_op jit(solution)/shard_map/ppermute | solution.py:13
  184.0 284.2 %copy-start = (bf16[16,128,256]{2,1,0:T(8,128)(2,1)S(1)}, bf16[16,128,256]{2,1,0:T(8,128)(2,1)}, u32[]{:S(2)}) copy-start(bf16[16,128,256]{2,1,0:T(8,128)(2,1)} %param.9) | copy-start | bytes 3145732
  186.6 281.6 %collective-permute-start.2 = (f32[16,128,256]{2,1,0:T(8,128)S(1)}, f32[16,128,256]{2,1,0:T(8,128)S(1)}, u32[]{:S(2)}, u32[]{:S(2)}) collective-permute-start(f32[16,128,256]{2,1,0:T(8,128)S(1)} %get-tuple-element.210), channel_id=1, source_target_pairs={{0,1},{1,2},{2,3},{3,4},{4,5},{5,6},{6,7},{7,8},{8,9},{9,10},{10,1... | collective-permute-start | bytes 6291464 | tf_op jit(solution)/shard_map/ppermute | solution.py:13
  214.4 253.8 %collective-permute-start.3 = (f32[16,128,256]{2,1,0:T(8,128)S(1)}, f32[16,128,256]{2,1,0:T(8,128)S(1)}, u32[]{:S(2)}, u32[]{:S(2)}) collective-permute-start(f32[16,128,256]{2,1,0:T(8,128)S(1)} %get-tuple-element.211), channel_id=1, source_target_pairs={{0,2},{1,3},{2,4},{3,5},{4,6},{5,7},{6,8},{7,9},{8,10},{9,11},{10,... | collective-permute-start | bytes 6291464 | tf_op jit(solution)/shard_map/ppermute | solution.py:13
  216.3 251.8 %collective-permute-start.4 = (f32[16,128]{1,0:T(8,128)S(1)}, f32[16,128]{1,0:T(8,128)S(1)}, u32[]{:S(2)}, u32[]{:S(2)}) collective-permute-start(f32[16,128]{1,0:T(8,128)S(1)} %get-tuple-element.214), channel_id=1, source_target_pairs={{0,1},{1,2},{2,3},{3,4},{4,5},{5,6},{6,7},{7,8},{8,9},{9,10},{10,1... | collective-permute-start | bytes 24584 | tf_op jit(solution)/shard_map/ppermute | solution.py:13
  218.3 249.9 %collective-permute-start.5 = (f32[16,128]{1,0:T(8,128)S(1)}, f32[16,128]{1,0:T(8,128)S(1)}, u32[]{:S(2)}, u32[]{:S(2)}) collective-permute-start(f32[16,128]{1,0:T(8,128)S(1)} %get-tuple-element.215), channel_id=1, source_target_pairs={{0,2},{1,3},{2,4},{3,5},{4,6},{5,7},{6,8},{7,9},{8,10},{9,11},{10,... | collective-permute-start | bytes 24584 | tf_op jit(solution)/shard_map/ppermute | solution.py:13
  470.4 25.8 %collective-permute-start.7 = (bf16[16,128,256]{2,1,0:T(8,128)(2,1)S(1)}, bf16[16,128,256]{2,1,0:T(8,128)(2,1)S(1)}, u32[]{:S(2)}, u32[]{:S(2)}) collective-permute-start(bf16[16,128,256]{2,1,0:T(8,128)(2,1)S(1)} %divide_convert_fusion.1), channel_id=1, source_target_pairs={{2,0},{3,1},{4,2},{5,3},{6,4},{7,5},{8,6},{9,7},{10,8},{11,9},{12,... | collective-permute-start | bytes 3145736 | tf_op jit(solution)/shard_map/ppermute | solution.py:13
  472.3 40.1 %collective-permute-start.6 = (bf16[16,128,256]{2,1,0:T(8,128)(2,1)S(1)}, bf16[16,128,256]{2,1,0:T(8,128)(2,1)S(1)}, u32[]{:S(2)}, u32[]{:S(2)}) collective-permute-start(bf16[16,128,256]{2,1,0:T(8,128)(2,1)S(1)} %divide_convert_fusion.1), channel_id=1, source_target_pairs={{1,0},{2,1},{3,2},{4,3},{5,4},{6,5},{7,6},{8,7},{9,8},{10,9},{11,1... | collective-permute-start | bytes 3145736 | tf_op jit(solution)/shard_map/ppermute | solution.py:13
  627.1 260.1 %collective-permute-start.8 = (f32[16,128,256]{2,1,0:T(8,128)S(1)}, f32[16,128,256]{2,1,0:T(8,128)S(1)}, u32[]{:S(2)}, u32[]{:S(2)}) collective-permute-start(f32[16,128,256]{2,1,0:T(8,128)S(1)} %get-tuple-element.208), channel_id=1, source_target_pairs={{0,1},{1,2},{2,3},{3,4},{4,5},{5,6},{6,7},{7,8},{8,9},{9,10},{10,1... | collective-permute-start | bytes 6291464 | tf_op jit(solution)/shard_map/ppermute | solution.py:13
  679.4 207.9 %collective-permute-start.9 = (f32[16,128,256]{2,1,0:T(8,128)S(1)}, f32[16,128,256]{2,1,0:T(8,128)S(1)}, u32[]{:S(2)}, u32[]{:S(2)}) collective-permute-start(f32[16,128,256]{2,1,0:T(8,128)S(1)} %get-tuple-element.209), channel_id=1, source_target_pairs={{0,2},{1,3},{2,4},{3,5},{4,6},{5,7},{6,8},{7,9},{8,10},{9,11},{10,... | collective-permute-start | bytes 6291464 | tf_op jit(solution)/shard_map/ppermute | solution.py:13
  681.3 205.9 %collective-permute-start.10 = (f32[16,128]{1,0:T(8,128)S(1)}, f32[16,128]{1,0:T(8,128)S(1)}, u32[]{:S(2)}, u32[]{:S(2)}) collective-permute-start(f32[16,128]{1,0:T(8,128)S(1)} %get-tuple-element.212), channel_id=1, source_target_pairs={{0,1},{1,2},{2,3},{3,4},{4,5},{5,6},{6,7},{7,8},{8,9},{9,10},{10,1... | collective-permute-start | bytes 24584 | tf_op jit(solution)/shard_map/ppermute | solution.py:13
  683.2 204.0 %collective-permute-start.11 = (f32[16,128]{1,0:T(8,128)S(1)}, f32[16,128]{1,0:T(8,128)S(1)}, u32[]{:S(2)}, u32[]{:S(2)}) collective-permute-start(f32[16,128]{1,0:T(8,128)S(1)} %get-tuple-element.213), channel_id=1, source_target_pairs={{0,2},{1,3},{2,4},{3,5},{4,6},{5,7},{6,8},{7,9},{8,10},{9,11},{10,... | collective-permute-start | bytes 24584 | tf_op jit(solution)/shard_map/ppermute | solution.py:13
where the time goes:
time: 895 us; the launch traced here: 890 us
  waiting for transfers between devices  535 us (60%)
  other arithmetic  137 us (15%)
  starting transfers between devices  119 us (13%)
  local copies, waits for them, and re-layouts  79.2 us (9%)
  matrix products  19.1 us (2%)
    ppermute x12, waiting for transfers between devices, passed_along(): return lax.ppermute(block, axis, route)  535 us
    ppermute x12, starting transfers between devices, passed_along(): return lax.ppermute(block, axis, route)  119 us
    scatter-add x18, other arithmetic, advance(): numerator = numerator.at[both_rows].add(terms)  80.7 us
    gather x18, local copies, waits for them, and re-layouts, advance(): picked = jnp.take(window, both_rows, axis=0)  50.4 us
  transfers between devices with their start and end apart: 12, of which 6 were waited for; matrix products, arithmetic and copies ran while one was open for 0% of the time, Pallas kernels for 0%

commit v1 on v0

v1 whole, which is shorter than its diff:
```python
import functools
import math

import jax
import jax.numpy as jnp
from jax import lax
from jax.experimental import pallas as pl
from jax.experimental.pallas import tpu as pltpu
from jax.sharding import PartitionSpec as P

MESH = pl.DeviceIdType.MESH
ROUNDS = 2
OWN, NEXT, PREV, NEXT2, PREV2 = range(5)
CHUNKS = 8
GROUP = 4


def split(square):
    high = square.astype(jnp.bfloat16)
    low = (square - high.astype(jnp.float32)).astype(jnp.bfloat16)
    return high, low


def squares(block):
    wide = block.astype(jnp.float32)
    return split(wide * wide)


def contract(a, b, da, db):
    return lax.dot_general(
        a, b, (((da,), (db,)), ((), ())), preferred_element_type=jnp.float32
    )


def kernel(
    shape,
    sizes,
    count_ref,
    pairs_ref,
    patches_ref,
    out_ref,
    window,
    numer,
    denom,
    target_power,
    source_row,
    extra,
    listed,
    block_send,
    block_recv,
    listed_send,
    listed_recv,
):
    outer, inner = shape
    leaves, points = sizes
    devices = outer * inner
    rows = leaves * points
    chunk = rows // CHUNKS
    width = GROUP * points
    groups = leaves // GROUP
    per_group = CHUNKS // groups
    spread = patches_ref.shape[1] / 4.0
    scale = math.log2(math.e) / spread
    me = lax.axis_index("gz") * inner + lax.axis_index("xy")

    def device(step):
        index = lax.rem(me + step + devices, devices)
        return (index // inner, lax.rem(index, inner))

    barrier = pltpu.get_barrier_semaphore()
    for step in (1, -1, 2, -2):
        pl.semaphore_signal(barrier, inc=1, device_id=device(step), device_id_type=MESH)

    def block_copy(turn, slot, piece, step):
        place = pl.ds(pl.multiple_of(piece * chunk, chunk), chunk)
        source = {1: OWN, -1: OWN, 2: PREV, -2: NEXT}[step]
        toward = 1 if step > 0 else -1
        return pltpu.make_async_remote_copy(
            src_ref=window.at[turn, source, place],
            dst_ref=window.at[turn, slot, place],
            send_sem=block_send.at[turn, slot, piece],
            recv_sem=block_recv.at[turn, slot, piece],
            device_id=device(toward),
            device_id_type=MESH,
        )

    def to_next(turn, piece):
        return block_copy(turn, PREV, piece, 1)

    def to_prev(turn, piece):
        return block_copy(turn, NEXT, piece, -1)

    def on_to_next(turn, piece):
        return block_copy(turn, PREV2, piece, 2)

    def on_to_prev(turn, piece):
        return block_copy(turn, NEXT2, piece, -2)

    window[0, OWN] = patches_ref[...]
    pl.semaphore_wait(barrier, 4)

    def send_own(turn):
        def body(piece, _):
            to_next(turn, piece).start()
            to_prev(turn, piece).start()
            return 0

        lax.fori_loop(0, CHUNKS, body, 0)

    send_own(0)

    slots = pairs_ref.shape[0]
    lanes = 128
    lane = lax.broadcasted_iota(jnp.int32, (slots, lanes), 1)
    live = lax.broadcasted_iota(jnp.int32, (slots, lanes), 0) < count_ref[me]
    first = jnp.where(live & (pairs_ref[:, 0:1] - me * leaves == lane), 1.0, 0.0)
    second = jnp.where(live & (pairs_ref[:, 1:2] - me * leaves == lane), 1.0, 0.0)
    first, second = first.astype(jnp.bfloat16), second.astype(jnp.bfloat16)
    forward = contract(first, second, 0, 0)
    backward = contract(second, first, 0, 0)
    listed[0] = backward[leaves : 2 * leaves]
    listed[1] = backward[2 * leaves : 3 * leaves]

    def listed_copy(k):
        return pltpu.make_async_remote_copy(
            src_ref=listed.at[k],
            dst_ref=listed.at[2 + k],
            send_sem=listed_send.at[k],
            recv_sem=listed_recv.at[k],
            device_id=device(k + 1),
            device_id_type=MESH,
        )

    for k in range(2):
        listed_copy(k).start()

    def expand(counts, base):
        place = lax.broadcasted_iota(jnp.int32, (lanes, rows), 0) - base
        owner = lax.broadcasted_iota(jnp.int32, (lanes, rows), 1) // points
        spots = jnp.where(place == owner, 1.0, 0.0).astype(jnp.bfloat16)
        wide = contract(counts.astype(jnp.bfloat16), spots, 1, 0)
        return jnp.where(wide > 0.0, jnp.log2(wide), -jnp.inf)

    ahead = forward[:leaves]
    extra[OWN] = expand(ahead + backward[:leaves], 0)
    extra[NEXT] = expand(ahead, leaves)
    extra[NEXT2] = expand(ahead, 2 * leaves)
    for k in range(2):
        listed_copy(k).wait()
    extra[PREV] = expand(listed[2], 0)
    extra[PREV2] = expand(listed[3], 0)

    def unit(turn, slot, group):
        place = pl.ds(pl.multiple_of(group * width, width), width)
        source = window[turn, slot, place, :]
        high, low = squares(source)
        ones = jnp.ones((8, source.shape[1]), jnp.bfloat16)
        power = contract(ones, high, 1, 1) + contract(ones, low, 1, 1)
        source_row[...] = power[0:1] * scale - extra[slot, :, place]
        cross = contract(window[turn, OWN], source, 1, 1)
        parts = []
        for t in range(leaves):
            span = slice(t * points, (t + 1) * points)
            total, part = None, []
            for s in range(GROUP):
                lanes_here = slice(s * points, (s + 1) * points)
                away = target_power[span, :] + source_row[t : t + 1, lanes_here]
                weight = jnp.exp2(cross[span, lanes_here] * (2.0 * scale) - away)
                total = weight if total is None else total + weight
                part.append(weight.astype(jnp.bfloat16))
            denom[span, :] += total
            parts.append(jnp.concatenate(part, axis=1))
        weights = jnp.concatenate(parts, axis=0)
        numer[...] += jnp.dot(weights, source, preferred_element_type=jnp.float32)

    def one_round(turn, _):
        high, low = squares(window[turn, OWN])
        ones = jnp.ones((high.shape[1], points), jnp.bfloat16)
        target_power[...] = scale * (contract(high, ones, 1, 0) + contract(low, ones, 1, 0))
        numer[...] = jnp.zeros_like(numer)
        denom[...] = jnp.zeros_like(denom)

        def near(group, _):
            def arrive(k, _):
                piece = group * per_group + k
                to_next(turn, piece).wait_recv()
                on_to_next(turn, piece).start()
                to_prev(turn, piece).wait_recv()
                on_to_prev(turn, piece).start()
                return 0

            unit(turn, OWN, group)
            lax.fori_loop(0, per_group, arrive, 0)

            def each(k, _):
                unit(turn, NEXT + k, group)
                return 0

            lax.fori_loop(0, 2, each, 0)
            return 0

        def far(group, _):
            def arrive(k, _):
                piece = group * per_group + k
                on_to_next(turn, piece).wait_recv()
                on_to_prev(turn, piece).wait_recv()
                return 0

            lax.fori_loop(0, per_group, arrive, 0)

            def each(k, _):
                unit(turn, NEXT2 + k, group)
                return 0

            lax.fori_loop(0, 2, each, 0)
            return 0

        lax.fori_loop(0, groups, near, 0)
        lax.fori_loop(0, groups, far, 0)

        def finish(piece, _):
            place = pl.ds(pl.multiple_of(piece * chunk, chunk), chunk)
            below = 1.0 + jnp.sum(denom[place, :], axis=1, keepdims=True)
            above = window[turn, OWN, place, :].astype(jnp.float32) + numer[place, :]
            out_ref[place, :] = (above * (1.0 / below)).astype(jnp.bfloat16)

            @pl.when(turn + 1 < ROUNDS)
            def _():
                window[1, OWN, place, :] = out_ref[place, :]
                to_next(1, piece).start()
                to_prev(1, piece).start()

            return 0

        lax.fori_loop(0, CHUNKS, finish, 0)
        return 0

    lax.fori_loop(0, ROUNDS, one_round, 0)

    def drain(piece, _):
        for turn in range(ROUNDS):
            for copy in (to_next, to_prev, on_to_next, on_to_prev):
                copy(turn, piece).wait_send()
        return 0

    lax.fori_loop(0, CHUNKS, drain, 0)


def solution(mesh):
    shape = (mesh.shape["gz"], mesh.shape["xy"])

    def on_device(patches, pair_leaves, pair_count):
        leaves, points, values = patches.shape
        rows = leaves * points
        vmem = pl.BlockSpec(memory_space=pltpu.VMEM)
        out = pl.pallas_call(
            functools.partial(kernel, shape, (leaves, points)),
            out_shape=jax.ShapeDtypeStruct((rows, values), jnp.bfloat16),
            in_specs=[pl.BlockSpec(memory_space=pltpu.SMEM), vmem, vmem],
            out_specs=vmem,
            scratch_shapes=[
                pltpu.VMEM((ROUNDS, 5, rows, values), jnp.bfloat16),
                pltpu.VMEM((rows, values), jnp.float32),
                pltpu.VMEM((rows, points), jnp.float32),
                pltpu.VMEM((rows, points), jnp.float32),
                pltpu.VMEM((leaves, GROUP * points), jnp.float32),
                pltpu.VMEM((5, leaves, rows), jnp.float32),
                pltpu.VMEM((4, leaves, 128), jnp.float32),
                pltpu.SemaphoreType.DMA((ROUNDS, 5, CHUNKS)),
                pltpu.SemaphoreType.DMA((ROUNDS, 5, CHUNKS)),
                pltpu.SemaphoreType.DMA((2,)),
                pltpu.SemaphoreType.DMA((2,)),
            ],
            compiler_params=pltpu.CompilerParams(
                collective_id=0, has_side_effects=True, vmem_limit_bytes=56 << 20
            ),
            name="denoise",
        )(pair_count, pair_leaves, patches.reshape(rows, values))
        return out.reshape(leaves, points, values)

    return jax.shard_map(
        on_device,
        mesh=mesh,
        in_specs=(P(("gz", "xy"), None, None), P(("gz", "xy"), None), P()),
        out_specs=P(("gz", "xy"), None, None),
        check_vma=False,
    )
```

time: 895 us -> 134 us (0.15)
  the two profiles are of different devices: /device:TPU:17 before, /device:TPU:1 now
where the time goes in v1:
time: 134 us
  Pallas kernels  130 us (97%)
  local copies, waits for them, and re-layouts  3.73 us (3%)
    pallas_call x1, Pallas kernels, on_device(): pl.pallas_call(functools.partial(kernel, shape, (leaves, points)), out_sh...  130 us
    unnamed x2, local copies, waits for them, and re-layouts  3.73 us

profile of v1, /device:TPU:1, one launch (start us, length us, event | category | flops | bytes accessed | tf_op | source)
XLA Modules:
  0.0 133.6 jit_solution(9326905377990123538)
XLA Ops:
  0.0 1.4 %copy.4.pairs_ref = s32[192,2]{1,0:T(8,128)} copy(s32[192,2]{0,1:T(2,128)} %param.4) | data formatting | bytes 3072 | tf_op args[1]
  1.4 129.8 %denoise.1 = bf16[2048,256]{1,0:T(8,128)(2,1)} custom-call(s32[128]{0:T(128)} %count_ref.1, s32[192,2]{1,0:T(8,128)} %copy.4.pairs_ref, bf16[2048,256]{1,0:T(8,128)(2,1)} %bitcast.3), custom_call_target="tpu_custom_call" | custom-call | tf_op jit(solution)/shard_map/denoise/pallas_call | solution.py:256
  131.3 2.3 %copy.6 = bf16[16,128,256]{2,1,0:T(8,128)(2,1)} copy(bf16[16,128,256]{2,1,0:T(8,128)(2,1)} %bitcast.2) | data formatting | bytes 2097152

commit v2 on v1

v2 whole, which is shorter than its diff:
```python
import functools
import math

import jax
import jax.numpy as jnp
from jax import lax
from jax.experimental import pallas as pl
from jax.experimental.pallas import tpu as pltpu
from jax.sharding import PartitionSpec as P

MESH = pl.DeviceIdType.MESH
ROUNDS = 2
RING = 4
PIECES = 8
BATCH = 2
HALF = PIECES // 2
PART = 2
OWN, RIGHT, LEFT, ACROSS, SIDE_A, SIDE_B, TRANSIT = range(7)
STAY, NEXT, PREV, NEXT2, PREV2 = range(5)
FIRST_AT = (2, 2, 1, 2, 1, 1, 1, 2, 8)
FIRST = (
    ((OWN, 0), (OWN, 1)), ((OWN, 2), (OWN, 3)), ((RIGHT, 4), (OWN, 4)), ((OWN, 5), (OWN, 6)),
    ((RIGHT, 5), (SIDE_A, 0)), ((ACROSS, 0), (ACROSS, 4)), ((SIDE_A, 1), (OWN, 7)), ((ACROSS, 1), (ACROSS, 5)),
    ((SIDE_B, 0), (RIGHT, 6)), ((SIDE_B, 4), (RIGHT, 7)), ((SIDE_B, 1), (ACROSS, 2)), ((ACROSS, 6), (SIDE_B, 5)),
    ((ACROSS, 3), (ACROSS, 7)), ((SIDE_A, 2), (RIGHT, 0)), ((SIDE_A, 4), (SIDE_A, 3)), ((RIGHT, 1), (SIDE_A, 5)),
    ((SIDE_B, 2), (RIGHT, 2)), ((SIDE_A, 6), (SIDE_B, 6)), ((RIGHT, 3), (SIDE_A, 7)), ((SIDE_B, 3), (SIDE_B, 7)),
)
INNER_AT = (2, 2, 2, 1, 1, 2, 1, 2, 7)
INNER = (
    ((OWN, 0), (OWN, 1)), ((OWN, 2), (OWN, 3)), ((RIGHT, 4), (LEFT, 0)), ((OWN, 4), (OWN, 5)),
    ((RIGHT, 5), (LEFT, 1)), ((OWN, 6), (OWN, 7)), ((ACROSS, 0), (ACROSS, 4)), ((ACROSS, 1), (ACROSS, 5)),
    ((SIDE_A, 0), (RIGHT, 6)), ((LEFT, 2), (SIDE_A, 4)), ((RIGHT, 7), (LEFT, 3)), ((SIDE_A, 1), (ACROSS, 2)),
    ((ACROSS, 6), (SIDE_A, 5)), ((ACROSS, 3), (ACROSS, 7)), ((SIDE_A, 2), (RIGHT, 0)), ((LEFT, 4), (SIDE_A, 6)),
    ((RIGHT, 1), (LEFT, 5)), ((SIDE_A, 3), (RIGHT, 2)), ((LEFT, 6), (SIDE_A, 7)), ((RIGHT, 3), (LEFT, 7)),
)
LAST_AT = FIRST_AT
LAST = tuple(
    tuple(
        (LEFT if block == RIGHT else block, part if block == OWN else (part + 4) % 8)
        for block, part in unit
    )
    for unit in FIRST
)


def chosen(values, index):
    result = values[0]
    for k in range(1, len(values)):
        if values[k] is not values[0]:
            result = jnp.where(index == k, values[k], result)
    return result


def split(square):
    high = square.astype(jnp.bfloat16)
    low = (square - high.astype(jnp.float32)).astype(jnp.bfloat16)
    return high, low


def squares(block):
    wide = block.astype(jnp.float32)
    return split(wide * wide)


def contract(a, b, da, db):
    return lax.dot_general(
        a, b, (((da,), (db,)), ((), ())), preferred_element_type=jnp.float32
    )


def kernel(
    shape,
    sizes,
    count_ref,
    pairs_ref,
    patches_ref,
    out_ref,
    window,
    numer,
    denom,
    target_power,
    source_row,
    extra,
    listed,
    block_send,
    block_recv,
    listed_send,
    listed_recv,
):
    outer, inner = shape
    leaves, points = sizes
    devices = outer * inner
    rows = leaves * points
    chunk = rows // PIECES
    width = PART * points
    parts_here = leaves // PART
    per_part = PIECES // parts_here
    spread = patches_ref.shape[1] / 4.0
    scale = math.log2(math.e) / spread
    me = lax.axis_index("gz") * inner + lax.axis_index("xy")
    row, z = me // RING, lax.rem(me, RING)

    def device(step):
        index = lax.rem(me + step + devices, devices)
        return (index // inner, lax.rem(index, inner))

    def along(step):
        index = row * RING + lax.rem(z + step + RING, RING)
        return (index // inner, lax.rem(index, inner))

    right, left = along(1), along(-1)
    up, down = device(RING), device(-RING)
    first, last = z == 0, z == RING - 1
    edge = first | last
    toward = lax.rem(me + jnp.where(z < 2, RING, -RING) + devices, devices)
    over = (toward // inner, lax.rem(toward, inner))

    barrier = pltpu.get_barrier_semaphore()
    peers = (right, left, up, down, device(1), device(-1), device(2), device(-2))
    for peer in peers:
        pl.semaphore_signal(barrier, inc=1, device_id=peer, device_id_type=MESH)

    def moved(turn, flow, source, slot, piece, target):
        place = pl.ds(pl.multiple_of(piece * chunk, chunk), chunk)
        return pltpu.make_async_remote_copy(
            src_ref=window.at[turn, source, place],
            dst_ref=window.at[turn, slot, place],
            send_sem=block_send.at[turn, flow, piece],
            recv_sem=block_recv.at[turn, slot, piece],
            device_id=target,
            device_id_type=MESH,
        )

    def arrived(turn, slot, piece):
        moved(turn, 0, OWN, slot, piece, right).wait_recv()

    def start(copy):
        copy.start()

    def finish_send(copy):
        copy.wait_send()

    def own_copies(turn, order, act):
        @pl.when((order < HALF) | jnp.logical_not(last))
        def _():
            act(moved(turn, 0, OWN, LEFT, order, right))

        @pl.when((order < HALF) | jnp.logical_not(first))
        def _():
            act(moved(turn, 1, OWN, RIGHT, lax.rem(order + HALF, PIECES), left))

    def transit_copies(turn, order, act):
        @pl.when(first)
        def _():
            act(moved(turn, 2, OWN, TRANSIT, order, down))

        @pl.when(last)
        def _():
            act(moved(turn, 2, OWN, TRANSIT, HALF + order, up))

    def ring_copies(turn, order, act):
        act(moved(turn, 3, LEFT, ACROSS, order, right))
        act(moved(turn, 3, RIGHT, ACROSS, HALF + order, left))

    def edge_copies(turn, order, act):
        @pl.when(first)
        def _():
            act(moved(turn, 4, LEFT, SIDE_A, order, up))

        @pl.when(last)
        def _():
            act(moved(turn, 4, RIGHT, SIDE_A, HALF + order, down))

    def over_copies(turn, order, act):
        for piece in (order, HALF + order):

            @pl.when(edge)
            def _():
                act(moved(turn, 5, ACROSS, SIDE_B, piece, over))

            @pl.when(jnp.logical_not(edge))
            def _():
                act(moved(turn, 5, ACROSS, SIDE_A, piece, over))

    def onward_copies(turn, order, act):
        @pl.when(first)
        def _():
            act(moved(turn, 6, TRANSIT, SIDE_A, order, left))

        @pl.when(last)
        def _():
            act(moved(turn, 6, TRANSIT, SIDE_A, HALF + order, right))

    def send_rest(turn, order):
        own_copies(turn, order, start)

        @pl.when(order >= HALF)
        def _():
            later = order - HALF

            @pl.when(first)
            def _():
                arrived(turn, TRANSIT, later)

            @pl.when(last)
            def _():
                arrived(turn, TRANSIT, order)

            onward_copies(turn, later, start)

    def transfers(turn, at):
        batch, place = (at - 1) // (2 * BATCH), lax.rem(at - 1, 2 * BATCH)
        order = BATCH * batch + lax.rem(place, BATCH)

        @pl.when((at > 0) & (place < BATCH))
        def _():
            arrived(turn, LEFT, order)
            arrived(turn, RIGHT, HALF + order)
            ring_copies(turn, order, start)
            edge_copies(turn, order, start)

        @pl.when((at > 0) & (place >= BATCH))
        def _():
            send_rest(turn, order + BATCH)
            arrived(turn, ACROSS, order)
            arrived(turn, ACROSS, HALF + order)
            over_copies(turn, order, start)

        @pl.when(at == PIECES)
        def _():
            for later in range(BATCH, HALF):
                send_rest(turn, HALF + later)

    window[0, OWN] = patches_ref[...]
    pl.semaphore_wait(barrier, len(peers))
    for order in range(BATCH):
        own_copies(0, order, start)

    def send_transit(order, _):
        transit_copies(0, order, start)
        return 0

    lax.fori_loop(0, HALF, send_transit, 0)

    slots = pairs_ref.shape[1]
    lanes = 128
    leaf = lax.broadcasted_iota(jnp.int32, (lanes, slots), 0) + me * leaves
    live = lax.broadcasted_iota(jnp.int32, (lanes, slots), 1) < count_ref[me]
    one_a = jnp.where(live & (pairs_ref[0:1, :] == leaf), 1.0, 0.0).astype(jnp.bfloat16)
    one_b = jnp.where(live & (pairs_ref[1:2, :] == leaf), 1.0, 0.0).astype(jnp.bfloat16)
    forward = contract(one_a, one_b, 1, 1)
    backward = contract(one_b, one_a, 1, 1)
    listed[0] = backward[leaves : 2 * leaves]
    listed[1] = backward[2 * leaves : 3 * leaves]

    def listed_copy(k):
        return pltpu.make_async_remote_copy(
            src_ref=listed.at[k],
            dst_ref=listed.at[2 + k],
            send_sem=listed_send.at[k],
            recv_sem=listed_recv.at[k],
            device_id=device(k + 1),
            device_id_type=MESH,
        )

    for k in range(2):
        listed_copy(k).start()

    def expand(counts, base):
        place = lax.broadcasted_iota(jnp.int32, (lanes, rows), 0) - base
        at = lax.broadcasted_iota(jnp.int32, (lanes, rows), 1) - place * points
        spots = jnp.where((at >= 0) & (at < points), 1.0, 0.0).astype(jnp.bfloat16)
        wide = contract(counts.astype(jnp.bfloat16), spots, 1, 0)
        return jnp.where(wide > 0.0, jnp.log2(wide), -jnp.inf)

    ahead = forward[:leaves]
    extra[STAY] = expand(ahead + backward[:leaves], 0)
    extra[NEXT] = expand(ahead, leaves)
    extra[NEXT2] = expand(ahead, 2 * leaves)
    for k in range(2):
        listed_copy(k).wait()
    extra[PREV] = expand(listed[2], 0)
    extra[PREV2] = expand(listed[3], 0)

    def unit(turn, number):
        sources, rows_here = [], []
        for half in range(2):
            codes = [
                jnp.where(
                    first,
                    8 * f[half][0] + f[half][1],
                    jnp.where(last, 8 * l[half][0] + l[half][1], 8 * i[half][0] + i[half][1]),
                )
                for f, i, l in zip(FIRST, INNER, LAST)
            ]
            code = chosen(codes, number)
            slot, part = code // 8, lax.rem(code, 8)
            side = (slot == SIDE_A) | (slot == SIDE_B)
            late = ((slot == LEFT) & (part >= 4)) | ((slot == RIGHT) & (part < 4))

            @pl.when(side | late)
            def _():
                for k in range(per_part):
                    arrived(turn, slot, part * per_part + k)

            near = jnp.where(first, PREV, jnp.where(z == 1, PREV2, jnp.where(last, NEXT, NEXT2)))
            far = jnp.where(z < 2, NEXT2, PREV2)
            beyond = jnp.where(first, PREV2, NEXT2)
            step = chosen((STAY, NEXT, PREV, far, near, beyond), slot)
            place = pl.ds(pl.multiple_of(part * width, width), width)
            sources.append(window[turn, slot, place, :])
            rows_here.append(extra[step, :, place])
        source = jnp.concatenate(sources, axis=0)
        high, low = squares(source)
        ones = jnp.ones((8, source.shape[1]), jnp.bfloat16)
        power = contract(ones, high, 1, 1) + contract(ones, low, 1, 1)
        source_row[...] = power[0:1] * scale - jnp.concatenate(rows_here, axis=1)
        cross = contract(window[turn, OWN], source, 1, 1)
        parts = []
        for t in range(leaves):
            span = slice(t * points, (t + 1) * points)
            total, part = None, []
            for s in range(2 * PART):
                lanes_here = slice(s * points, (s + 1) * points)
                away = target_power[span, :] + source_row[t : t + 1, lanes_here]
                weight = jnp.exp2(cross[span, lanes_here] * (2.0 * scale) - away)
                total = weight if total is None else total + weight
                part.append(weight.astype(jnp.bfloat16))
            denom[span, :] += total
            parts.append(jnp.concatenate(part, axis=1))
        weights = jnp.concatenate(parts, axis=0)
        numer[...] += jnp.dot(weights, source, preferred_element_type=jnp.float32)

    def one_round(turn, _):
        high, low = squares(window[turn, OWN])
        ones = jnp.ones((high.shape[1], points), jnp.bfloat16)
        target_power[...] = scale * (contract(high, ones, 1, 0) + contract(low, ones, 1, 0))
        numer[...] = jnp.zeros_like(numer)
        denom[...] = jnp.zeros_like(denom)

        def step(at, done):
            transfers(turn, at)
            more = chosen(
                [
                    jnp.where(first | last, e, i) if e != i else e
                    for e, i in zip(FIRST_AT, INNER_AT)
                ],
                at,
            )

            def each(k, _):
                unit(turn, done + k)
                return 0

            lax.fori_loop(0, more, each, 0)
            return done + more

        lax.fori_loop(0, len(FIRST_AT), step, 0)

        def finish(order, _):
            piece = order // 2 + HALF * lax.rem(order, 2)
            place = pl.ds(pl.multiple_of(piece * chunk, chunk), chunk)
            below = 1.0 + jnp.sum(denom[place, :], axis=1, keepdims=True)
            above = window[turn, OWN, place, :].astype(jnp.float32) + numer[place, :]
            out_ref[place, :] = (above * (1.0 / below)).astype(jnp.bfloat16)

            @pl.when(turn + 1 < ROUNDS)
            def _():
                window[1, OWN, place, :] = out_ref[place, :]

                @pl.when((lax.rem(order, 2) == 1) & (order // 2 < BATCH))
                def _():
                    own_copies(1, order // 2, start)

                @pl.when(lax.rem(order, 2) == 1)
                def _():
                    transit_copies(1, order // 2, start)

            return 0

        lax.fori_loop(0, PIECES, finish, 0)
        return 0

    lax.fori_loop(0, ROUNDS, one_round, 0)

    def drain(order, _):
        for turn in range(ROUNDS):
            own_copies(turn, order, finish_send)
            own_copies(turn, HALF + order, finish_send)
            for kind in (
                transit_copies,
                ring_copies,
                edge_copies,
                over_copies,
                onward_copies,
            ):
                kind(turn, order, finish_send)
        return 0

    lax.fori_loop(0, HALF, drain, 0)


def solution(mesh):
    shape = (mesh.shape["gz"], mesh.shape["xy"])

    def on_device(patches, pair_leaves, pair_count):
        leaves, points, values = patches.shape
        rows = leaves * points
        vmem = pl.BlockSpec(memory_space=pltpu.VMEM)
        out = pl.pallas_call(
            functools.partial(kernel, shape, (leaves, points)),
            out_shape=jax.ShapeDtypeStruct((rows, values), jnp.bfloat16),
            in_specs=[pl.BlockSpec(memory_space=pltpu.SMEM), vmem, vmem],
            out_specs=vmem,
            scratch_shapes=[
                pltpu.VMEM((ROUNDS, 7, rows, values), jnp.bfloat16),
                pltpu.VMEM((rows, values), jnp.float32),
                pltpu.VMEM((rows, points), jnp.float32),
                pltpu.VMEM((rows, points), jnp.float32),
                pltpu.VMEM((leaves, 2 * PART * points), jnp.float32),
                pltpu.VMEM((5, leaves, rows), jnp.float32),
                pltpu.VMEM((4, leaves, 128), jnp.float32),
                pltpu.SemaphoreType.DMA((ROUNDS, 7, PIECES)),
                pltpu.SemaphoreType.DMA((ROUNDS, 7, PIECES)),
                pltpu.SemaphoreType.DMA((2,)),
                pltpu.SemaphoreType.DMA((2,)),
            ],
            compiler_params=pltpu.CompilerParams(
                collective_id=0, has_side_effects=True, vmem_limit_bytes=56 << 20
            ),
            name="denoise",
        )(pair_count, pair_leaves.T, patches.reshape(rows, values))
        return out.reshape(leaves, points, values)

    return jax.shard_map(
        on_device,
        mesh=mesh,
        in_specs=(P(("gz", "xy"), None, None), P(("gz", "xy"), None), P()),
        out_specs=P(("gz", "xy"), None, None),
        check_vma=False,
    )
```

time: 134 us -> 122 us (0.910); the launches traced: 134 us -> 119 us
  Pallas kernels: 130 us -> 117 us
  local copies, waits for them, and re-layouts: 3.73 us -> 2.29 us
    pallas_call x1, Pallas kernels: 130 us -> 117 us  [on_device(): pl.pallas_call(functools.partial(kernel, shape, (leaves, points)), out_sh...]
    unnamed x2 -> x1, local copies, waits for them, and re-layouts: 3.73 us -> 2.29 us
where the time goes in v2:
time: 122 us; the launch traced here: 119 us
  Pallas kernels  117 us (96%)
  local copies, waits for them, and re-layouts  2.29 us (2%)
    pallas_call x1, Pallas kernels, on_device(): pl.pallas_call(functools.partial(kernel, shape, (leaves, points)), out_sh...  117 us

profile of v2, /device:TPU:1, one launch (start us, length us, event | category | flops | bytes accessed | tf_op | source)
XLA Modules:
  0.0 119.2 jit_solution(5122255260371657463)
XLA Ops:
  0.0 116.9 %denoise.1 = bf16[2048,256]{1,0:T(8,128)(2,1)} custom-call(s32[128]{0:T(128)} %count_ref.1, s32[2,192]{1,0:T(2,128)} %bitcast.5, bf16[2048,256]{1,0:T(8,128)(2,1)} %bitcast.4), custom_call_target="tpu_custom_call" | custom-call | tf_op jit(solution)/shard_map/denoise/pallas_call | solution.py:410
  116.9 2.3 %copy.5 = bf16[16,128,256]{2,1,0:T(8,128)(2,1)} copy(bf16[16,128,256]{2,1,0:T(8,128)(2,1)} %bitcast.3) | data formatting | bytes 2097152

commit v3 on v2

--- a/solution.py
+++ b/solution.py
@@ -13,24 +13,25 @@
 RING = 4
 PIECES = 8
 BATCH = 2
+SHIFT = 1
 HALF = PIECES // 2
 PART = 2
 OWN, RIGHT, LEFT, ACROSS, SIDE_A, SIDE_B, TRANSIT = range(7)
 STAY, NEXT, PREV, NEXT2, PREV2 = range(5)
-FIRST_AT = (2, 2, 1, 2, 1, 1, 1, 2, 8)
+FIRST_AT = (1, 2, 2, 1, 2, 1, 1, 1, 9)
 FIRST = (
-    ((OWN, 0), (OWN, 1)), ((OWN, 2), (OWN, 3)), ((RIGHT, 4), (OWN, 4)), ((OWN, 5), (OWN, 6)),
-    ((RIGHT, 5), (SIDE_A, 0)), ((ACROSS, 0), (ACROSS, 4)), ((SIDE_A, 1), (OWN, 7)), ((ACROSS, 1), (ACROSS, 5)),
-    ((SIDE_B, 0), (RIGHT, 6)), ((SIDE_B, 4), (RIGHT, 7)), ((SIDE_B, 1), (ACROSS, 2)), ((ACROSS, 6), (SIDE_B, 5)),
-    ((ACROSS, 3), (ACROSS, 7)), ((SIDE_A, 2), (RIGHT, 0)), ((SIDE_A, 4), (SIDE_A, 3)), ((RIGHT, 1), (SIDE_A, 5)),
-    ((SIDE_B, 2), (RIGHT, 2)), ((SIDE_A, 6), (SIDE_B, 6)), ((RIGHT, 3), (SIDE_A, 7)), ((SIDE_B, 3), (SIDE_B, 7)),
+    ((OWN, 0), (OWN, 1)), ((RIGHT, 4), (OWN, 2)), ((OWN, 3), (OWN, 4)), ((RIGHT, 5), (OWN, 5)),
+    ((OWN, 6), (OWN, 7)), ((SIDE_A, 0), (ACROSS, 0)), ((ACROSS, 4), (SIDE_A, 1)), ((ACROSS, 1), (ACROSS, 5)),
+    ((RIGHT, 6), (SIDE_B, 0)), ((RIGHT, 7), (SIDE_B, 4)), ((ACROSS, 6), (SIDE_B, 1)), ((ACROSS, 2), (ACROSS, 7)),
+    ((SIDE_B, 5), (ACROSS, 3)), ((RIGHT, 0), (SIDE_A, 2)), ((SIDE_A, 4), (RIGHT, 1)), ((SIDE_B, 2), (SIDE_A, 5)),
+    ((RIGHT, 2), (SIDE_B, 6)), ((SIDE_A, 6), (RIGHT, 3)), ((SIDE_B, 3), (SIDE_A, 7)), ((SIDE_B, 7), (SIDE_A, 3)),
 )
-INNER_AT = (2, 2, 2, 1, 1, 2, 1, 2, 7)
+INNER_AT = (1, 2, 2, 1, 2, 1, 2, 2, 7)
 INNER = (
-    ((OWN, 0), (OWN, 1)), ((OWN, 2), (OWN, 3)), ((RIGHT, 4), (LEFT, 0)), ((OWN, 4), (OWN, 5)),
-    ((RIGHT, 5), (LEFT, 1)), ((OWN, 6), (OWN, 7)), ((ACROSS, 0), (ACROSS, 4)), ((ACROSS, 1), (ACROSS, 5)),
-    ((SIDE_A, 0), (RIGHT, 6)), ((LEFT, 2), (SIDE_A, 4)), ((RIGHT, 7), (LEFT, 3)), ((SIDE_A, 1), (ACROSS, 2)),
-    ((ACROSS, 6), (SIDE_A, 5)), ((ACROSS, 3), (ACROSS, 7)), ((SIDE_A, 2), (RIGHT, 0)), ((LEFT, 4), (SIDE_A, 6)),
+    ((OWN, 0), (OWN, 1)), ((LEFT, 0), (RIGHT, 4)), ((OWN, 2), (OWN, 3)), ((LEFT, 1), (RIGHT, 5)),
+    ((OWN, 4), (OWN, 5)), ((ACROSS, 0), (ACROSS, 4)), ((ACROSS, 1), (ACROSS, 5)), ((OWN, 6), (OWN, 7)),
+    ((SIDE_A, 0), (LEFT, 2)), ((RIGHT, 6), (SIDE_A, 4)), ((RIGHT, 7), (LEFT, 3)), ((SIDE_A, 1), (ACROSS, 6)),
+    ((ACROSS, 2), (SIDE_A, 5)), ((ACROSS, 7), (ACROSS, 3)), ((SIDE_A, 2), (RIGHT, 0)), ((LEFT, 4), (SIDE_A, 6)),
     ((RIGHT, 1), (LEFT, 5)), ((SIDE_A, 3), (RIGHT, 2)), ((LEFT, 6), (SIDE_A, 7)), ((RIGHT, 3), (LEFT, 7)),
 )
 LAST_AT = FIRST_AT
@@ -149,25 +150,31 @@
         def _():
             act(moved(turn, 1, OWN, RIGHT, lax.rem(order + HALF, PIECES), left))
 
+    def passing(order):
+        at_last = jnp.where(order < HALF, HALF + order, order - SHIFT)
+        return lax.rem(at_last + HALF, PIECES), at_last
+
     def transit_copies(turn, order, act):
+        at_first, at_last = passing(order)
+
         @pl.when(first)
         def _():
-            act(moved(turn, 2, OWN, TRANSIT, order, down))
+            act(moved(turn, 2, OWN, TRANSIT, at_first, down))
 
         @pl.when(last)
         def _():
-            act(moved(turn, 2, OWN, TRANSIT, HALF + order, up))
+            act(moved(turn, 2, OWN, TRANSIT, at_last, up))
 
     def ring_copies(turn, order, act):
         act(moved(turn, 3, LEFT, ACROSS, order, right))
         act(moved(turn, 3, RIGHT, ACROSS, HALF + order, left))
 
     def edge_copies(turn, order, act):
-        @pl.when(first)
+        @pl.when(first & (order < HALF - SHIFT))
         def _():
             act(moved(turn, 4, LEFT, SIDE_A, order, up))
 
-        @pl.when(last)
+        @pl.when(last & (order < HALF - SHIFT))
         def _():
             act(moved(turn, 4, RIGHT, SIDE_A, HALF + order, down))
 
@@ -183,30 +190,35 @@
                 act(moved(turn, 5, ACROSS, SIDE_A, piece, over))
 
     def onward_copies(turn, order, act):
+        at_first, at_last = passing(order)
+
         @pl.when(first)
         def _():
-            act(moved(turn, 6, TRANSIT, SIDE_A, order, left))
+            act(moved(turn, 6, TRANSIT, SIDE_A, at_first, left))
 
         @pl.when(last)
         def _():
-            act(moved(turn, 6, TRANSIT, SIDE_A, HALF + order, right))
+            act(moved(turn, 6, TRANSIT, SIDE_A, at_last, right))
+
+    def pass_on(turn, order):
+        at_first, at_last = passing(order)
+
+        @pl.when(first)
+        def _():
+            arrived(turn, TRANSIT, at_first)
+
+        @pl.when(last)
+        def _():
+            arrived(turn, TRANSIT, at_last)
+
+        onward_copies(turn, order, start)
 
     def send_rest(turn, order):
         own_copies(turn, order, start)
 
         @pl.when(order >= HALF)
         def _():
-            later = order - HALF
-
-            @pl.when(first)
-            def _():
-                arrived(turn, TRANSIT, later)
-
-            @pl.when(last)
-            def _():
-                arrived(turn, TRANSIT, order)
-
-            onward_copies(turn, later, start)
+            pass_on(turn, order - HALF)
 
     def transfers(turn, at):
         batch, place = (at - 1) // (2 * BATCH), lax.rem(at - 1, 2 * BATCH)
@@ -230,6 +242,8 @@
         def _():
             for later in range(BATCH, HALF):
                 send_rest(turn, HALF + later)
+            for later in range(SHIFT):
+                pass_on(turn, HALF + later)
 
     window[0, OWN] = patches_ref[...]
     pl.semaphore_wait(barrier, len(peers))
@@ -240,7 +254,7 @@
         transit_copies(0, order, start)
         return 0
 
-    lax.fori_loop(0, HALF, send_transit, 0)
+    lax.fori_loop(0, HALF + SHIFT, send_transit, 0)
 
     slots = pairs_ref.shape[1]
     lanes = 128
@@ -266,21 +280,34 @@
     for k in range(2):
         listed_copy(k).start()
 
-    def expand(counts, base):
-        place = lax.broadcasted_iota(jnp.int32, (lanes, rows), 0) - base
-        at = lax.broadcasted_iota(jnp.int32, (lanes, rows), 1) - place * points
-        spots = jnp.where((at >= 0) & (at < points), 1.0, 0.0).astype(jnp.bfloat16)
-        wide = contract(counts.astype(jnp.bfloat16), spots, 1, 0)
-        return jnp.where(wide > 0.0, jnp.log2(wide), -jnp.inf)
-
+    def begin_round(turn):
+        high, low = squares(window[turn, OWN])
+        ones = jnp.ones((high.shape[1], points), jnp.bfloat16)
+        target_power[...] = scale * (contract(high, ones, 1, 0) + contract(low, ones, 1, 0))
+        numer[...] = jnp.zeros_like(numer)
+        denom[...] = jnp.zeros_like(denom)
+
+    begin_round(0)
     ahead = forward[:leaves]
-    extra[STAY] = expand(ahead + backward[:leaves], 0)
-    extra[NEXT] = expand(ahead, leaves)
-    extra[NEXT2] = expand(ahead, 2 * leaves)
     for k in range(2):
         listed_copy(k).wait()
-    extra[PREV] = expand(listed[2], 0)
-    extra[PREV2] = expand(listed[3], 0)
+    counts = jnp.concatenate(
+        [
+            ahead + backward[:leaves],
+            pltpu.roll(ahead, lanes - leaves, 1),
+            listed[2],
+            pltpu.roll(ahead, lanes - 2 * leaves, 1),
+            listed[3],
+        ],
+        axis=0,
+    )
+    place = lax.broadcasted_iota(jnp.int32, (lanes, rows), 0)
+    at = lax.broadcasted_iota(jnp.int32, (lanes, rows), 1) - place * points
+    spots = jnp.where((at >= 0) & (at < points), 1.0, 0.0).astype(jnp.bfloat16)
+    wide = contract(counts.astype(jnp.bfloat16), spots, 1, 0)
+    wide = jnp.where(wide > 0.0, jnp.log2(wide), -jnp.inf)
+    for k in range(5):
+        extra[k] = wide[k * leaves : (k + 1) * leaves]
 
     def unit(turn, number):
         sources, rows_here = [], []
@@ -311,10 +338,16 @@
             sources.append(window[turn, slot, place, :])
             rows_here.append(extra[step, :, place])
         source = jnp.concatenate(sources, axis=0)
-        high, low = squares(source)
-        ones = jnp.ones((8, source.shape[1]), jnp.bfloat16)
-        power = contract(ones, high, 1, 1) + contract(ones, low, 1, 1)
-        source_row[...] = power[0:1] * scale - jnp.concatenate(rows_here, axis=1)
+        wide = source.astype(jnp.float32)
+        wide = wide * wide
+        folded = wide[:, :points] + wide[:, points:]
+        power = [
+            jnp.sum(folded[s * points : (s + 1) * points].T, axis=0, keepdims=True)
+            for s in range(2 * PART)
+        ]
+        source_row[...] = jnp.concatenate(power, axis=1) * scale - jnp.concatenate(
+            rows_here, axis=1
+        )
         cross = contract(window[turn, OWN], source, 1, 1)
         parts = []
         for t in range(leaves):
@@ -332,11 +365,9 @@
         numer[...] += jnp.dot(weights, source, preferred_element_type=jnp.float32)
 
     def one_round(turn, _):
-        high, low = squares(window[turn, OWN])
-        ones = jnp.ones((high.shape[1], points), jnp.bfloat16)
-        target_power[...] = scale * (contract(high, ones, 1, 0) + contract(low, ones, 1, 0))
-        numer[...] = jnp.zeros_like(numer)
-        denom[...] = jnp.zeros_like(denom)
+        @pl.when(turn > 0)
+        def _():
+            begin_round(turn)
 
         def step(at, done):
             transfers(turn, at)
@@ -375,6 +406,11 @@
                 @pl.when(lax.rem(order, 2) == 1)
                 def _():
                     transit_copies(1, order // 2, start)
+
+                @pl.when(order == PIECES - 1)
+                def _():
+                    for later in range(SHIFT):
+                        transit_copies(1, HALF + later, start)
 
             return 0
 
@@ -398,6 +434,10 @@
         return 0
 
     lax.fori_loop(0, HALF, drain, 0)
+    for turn in range(ROUNDS):
+        for order in range(HALF, HALF + SHIFT):
+            transit_copies(turn, order, finish_send)
+            onward_copies(turn, order, finish_send)
 
 
 def solution(mesh):

time: 122 us -> 115 us (0.943); the launches traced: 119 us -> 115 us
  Pallas kernels: 117 us -> 112 us
    pallas_call x1, Pallas kernels: 117 us -> 112 us  [on_device(): pl.pallas_call(functools.partial(kernel, shape, (leaves, points)), out_sh...]
where the time goes in v3:
time: 115 us
  Pallas kernels  112 us (97%)
  local copies, waits for them, and re-layouts  2.29 us (2%)
    pallas_call x1, Pallas kernels, on_device(): pl.pallas_call(functools.partial(kernel, shape, (leaves, points)), out_sh...  112 us

profile of v3, /device:TPU:1, one launch (start us, length us, event | category | flops | bytes accessed | tf_op | source)
XLA Modules:
  0.0 114.5 jit_solution(5979768195115541193)
XLA Ops:
  0.0 112.2 %denoise.1 = bf16[2048,256]{1,0:T(8,128)(2,1)} custom-call(s32[128]{0:T(128)} %count_ref.1, s32[2,192]{1,0:T(2,128)} %bitcast.5, bf16[2048,256]{1,0:T(8,128)(2,1)} %bitcast.4), custom_call_target="tpu_custom_call" | custom-call | tf_op jit(solution)/shard_map/denoise/pallas_call | solution.py:450
  112.2 2.3 %copy.5 = bf16[16,128,256]{2,1,0:T(8,128)(2,1)} copy(bf16[16,128,256]{2,1,0:T(8,128)(2,1)} %bitcast.3) | data formatting | bytes 2097152

commit v4 on v3

--- a/solution.py
+++ b/solution.py
@@ -83,6 +83,9 @@
     source_row,
     extra,
     listed,
+    result,
+    load_sem,
+    store_sem,
     block_send,
     block_recv,
     listed_send,
@@ -116,6 +119,9 @@
     toward = lax.rem(me + jnp.where(z < 2, RING, -RING) + devices, devices)
     over = (toward // inner, lax.rem(toward, inner))
 
+    load = pltpu.make_async_copy(patches_ref, window.at[0, OWN], load_sem)
+    load.start()
+
     barrier = pltpu.get_barrier_semaphore()
     peers = (right, left, up, down, device(1), device(-1), device(2), device(-2))
     for peer in peers:
@@ -245,8 +251,8 @@
             for later in range(SHIFT):
                 pass_on(turn, HALF + later)
 
-    window[0, OWN] = patches_ref[...]
     pl.semaphore_wait(barrier, len(peers))
+    load.wait()
     for order in range(BATCH):
         own_copies(0, order, start)
 
@@ -280,6 +286,10 @@
     for k in range(2):
         listed_copy(k).start()
 
+    def store(piece):
+        place = pl.ds(pl.multiple_of(piece * chunk, chunk), chunk)
+        return pltpu.make_async_copy(result.at[place], out_ref.at[place], store_sem.at[piece])
+
     def begin_round(turn):
         high, low = squares(window[turn, OWN])
         ones = jnp.ones((high.shape[1], points), jnp.bfloat16)
@@ -287,27 +297,26 @@
         numer[...] = jnp.zeros_like(numer)
         denom[...] = jnp.zeros_like(denom)
 
+    def tabulate(counts, steps):
+        counts = jnp.concatenate(counts, axis=0).astype(jnp.bfloat16)
+        place = lax.broadcasted_iota(jnp.int32, (lanes, rows), 0)
+        at = lax.broadcasted_iota(jnp.int32, (lanes, rows), 1) - place * points
+        spots = jnp.where((at >= 0) & (at < points), 1.0, 0.0).astype(jnp.bfloat16)
+        wide = contract(counts, spots, 1, 0)
+        wide = jnp.where(wide > 0.0, jnp.log2(wide), -jnp.inf)
+        for k, step in enumerate(steps):
+            extra[step] = wide[k * leaves : (k + 1) * leaves]
+
     begin_round(0)
     ahead = forward[:leaves]
-    for k in range(2):
-        listed_copy(k).wait()
-    counts = jnp.concatenate(
+    tabulate(
         [
             ahead + backward[:leaves],
             pltpu.roll(ahead, lanes - leaves, 1),
-            listed[2],
             pltpu.roll(ahead, lanes - 2 * leaves, 1),
-            listed[3],
         ],
-        axis=0,
+        (STAY, NEXT, NEXT2),
     )
-    place = lax.broadcasted_iota(jnp.int32, (lanes, rows), 0)
-    at = lax.broadcasted_iota(jnp.int32, (lanes, rows), 1) - place * points
-    spots = jnp.where((at >= 0) & (at < points), 1.0, 0.0).astype(jnp.bfloat16)
-    wide = contract(counts.astype(jnp.bfloat16), spots, 1, 0)
-    wide = jnp.where(wide > 0.0, jnp.log2(wide), -jnp.inf)
-    for k in range(5):
-        extra[k] = wide[k * leaves : (k + 1) * leaves]
 
     def unit(turn, number):
         sources, rows_here = [], []
@@ -371,6 +380,13 @@
 
         def step(at, done):
             transfers(turn, at)
+
+            @pl.when((turn == 0) & (at == 1))
+            def _():
+                for k in range(2):
+                    listed_copy(k).wait()
+                tabulate([listed[2], listed[3]], (PREV, PREV2))
+
             more = chosen(
                 [
                     jnp.where(first | last, e, i) if e != i else e
@@ -393,11 +409,15 @@
             place = pl.ds(pl.multiple_of(piece * chunk, chunk), chunk)
             below = 1.0 + jnp.sum(denom[place, :], axis=1, keepdims=True)
             above = window[turn, OWN, place, :].astype(jnp.float32) + numer[place, :]
-            out_ref[place, :] = (above * (1.0 / below)).astype(jnp.bfloat16)
+            result[place, :] = (above * (1.0 / below)).astype(jnp.bfloat16)
+
+            @pl.when(turn + 1 == ROUNDS)
+            def _():
+                store(piece).start()
 
             @pl.when(turn + 1 < ROUNDS)
             def _():
-                window[1, OWN, place, :] = out_ref[place, :]
+                window[1, OWN, place, :] = result[place, :]
 
                 @pl.when((lax.rem(order, 2) == 1) & (order // 2 < BATCH))
                 def _():
@@ -420,6 +440,8 @@
     lax.fori_loop(0, ROUNDS, one_round, 0)
 
     def drain(order, _):
+        store(order).wait()
+        store(HALF + order).wait()
         for turn in range(ROUNDS):
             own_copies(turn, order, finish_send)
             own_copies(turn, HALF + order, finish_send)
@@ -447,11 +469,12 @@
         leaves, points, values = patches.shape
         rows = leaves * points
         vmem = pl.BlockSpec(memory_space=pltpu.VMEM)
+        anywhere = pl.BlockSpec(memory_space=pl.ANY)
         out = pl.pallas_call(
             functools.partial(kernel, shape, (leaves, points)),
             out_shape=jax.ShapeDtypeStruct((rows, values), jnp.bfloat16),
-            in_specs=[pl.BlockSpec(memory_space=pltpu.SMEM), vmem, vmem],
-            out_specs=vmem,
+            in_specs=[pl.BlockSpec(memory_space=pltpu.SMEM), vmem, anywhere],
+            out_specs=anywhere,
             scratch_shapes=[
                 pltpu.VMEM((ROUNDS, 7, rows, values), jnp.bfloat16),
                 pltpu.VMEM((rows, values), jnp.float32),
@@ -460,6 +483,9 @@
                 pltpu.VMEM((leaves, 2 * PART * points), jnp.float32),
                 pltpu.VMEM((5, leaves, rows), jnp.float32),
                 pltpu.VMEM((4, leaves, 128), jnp.float32),
+                pltpu.VMEM((rows, values), jnp.bfloat16),
+                pltpu.SemaphoreType.DMA,
+                pltpu.SemaphoreType.DMA((PIECES,)),
                 pltpu.SemaphoreType.DMA((ROUNDS, 7, PIECES)),
                 pltpu.SemaphoreType.DMA((ROUNDS, 7, PIECES)),
                 pltpu.SemaphoreType.DMA((2,)),

time: 115 us -> 112 us (0.974)
  Pallas kernels: 112 us -> 109 us
    pallas_call x1, Pallas kernels: 112 us -> 109 us  [on_device(): pl.pallas_call(functools.partial(kernel, shape, (leaves, points)), out_sh...]
where the time goes in v4:
time: 112 us
  Pallas kernels  109 us (97%)
  local copies, waits for them, and re-layouts  2.29 us (2%)
    pallas_call x1, Pallas kernels, on_device(): pl.pallas_call(functools.partial(kernel, shape, (leaves, points)), out_sh...  109 us
    unnamed x1, local copies, waits for them, and re-layouts  2.29 us

profile of v4, /device:TPU:1, one launch (start us, length us, event | category | flops | bytes accessed | tf_op | source)
XLA Modules:
  0.0 111.6 jit_solution(11222242918366431440)
XLA Ops:
  0.0 109.3 %denoise.1 = bf16[2048,256]{1,0:T(8,128)(2,1)} custom-call(s32[128]{0:T(128)} %count_ref.1, s32[2,192]{1,0:T(2,128)} %bitcast.5, bf16[2048,256]{1,0:T(8,128)(2,1)} %bitcast.4), custom_call_target="tpu_custom_call" | custom-call | tf_op jit(solution)/shard_map/denoise/pallas_call | solution.py:473
  109.3 2.3 %copy.5 = bf16[16,128,256]{2,1,0:T(8,128)(2,1)} copy(bf16[16,128,256]{2,1,0:T(8,128)(2,1)} %bitcast.3) | data formatting | bytes 2097152

commit v5 on v4

--- a/solution.py
+++ b/solution.py
@@ -405,36 +405,37 @@
         lax.fori_loop(0, len(FIRST_AT), step, 0)
 
         def finish(order, _):
-            piece = order // 2 + HALF * lax.rem(order, 2)
-            place = pl.ds(pl.multiple_of(piece * chunk, chunk), chunk)
-            below = 1.0 + jnp.sum(denom[place, :], axis=1, keepdims=True)
-            above = window[turn, OWN, place, :].astype(jnp.float32) + numer[place, :]
-            result[place, :] = (above * (1.0 / below)).astype(jnp.bfloat16)
+            for piece in (order, HALF + order):
+                place = pl.ds(pl.multiple_of(piece * chunk, chunk), chunk)
+                below = 1.0 + jnp.sum(denom[place, :], axis=1, keepdims=True)
+                above = window[turn, OWN, place, :].astype(jnp.float32) + numer[place, :]
+                result[place, :] = (above * (1.0 / below)).astype(jnp.bfloat16)
 
             @pl.when(turn + 1 == ROUNDS)
             def _():
-                store(piece).start()
+                store(order).start()
+                store(HALF + order).start()
 
             @pl.when(turn + 1 < ROUNDS)
             def _():
-                window[1, OWN, place, :] = result[place, :]
-
-                @pl.when((lax.rem(order, 2) == 1) & (order // 2 < BATCH))
+                for piece in (order, HALF + order):
+                    place = pl.ds(pl.multiple_of(piece * chunk, chunk), chunk)
+                    window[1, OWN, place, :] = result[place, :]
+
+                @pl.when(order < BATCH)
                 def _():
-                    own_copies(1, order // 2, start)
-
-                @pl.when(lax.rem(order, 2) == 1)
-                def _():
-                    transit_copies(1, order // 2, start)
-
-                @pl.when(order == PIECES - 1)
+                    own_copies(1, order, start)
+
+                transit_copies(1, order, start)
+
+                @pl.when(order == HALF - 1)
                 def _():
                     for later in range(SHIFT):
                         transit_copies(1, HALF + later, start)
 
             return 0
 
-        lax.fori_loop(0, PIECES, finish, 0)
+        lax.fori_loop(0, HALF, finish, 0)
         return 0
 
     lax.fori_loop(0, ROUNDS, one_round, 0)

time: 112 us -> 111 us (level)
  no operation moved by 1% of the time
where the time goes in v5:
time: 111 us
  Pallas kernels  109 us (98%)
  local copies, waits for them, and re-layouts  2.29 us (2%)
    pallas_call x1, Pallas kernels, on_device(): pl.pallas_call(functools.partial(kernel, shape, (leaves, points)), out_sh...  109 us
    unnamed x1, local copies, waits for them, and re-layouts  2.29 us

profile of v5, /device:TPU:1, one launch (start us, length us, event | category | flops | bytes accessed | tf_op | source)
XLA Modules:
  0.0 111.2 jit_solution(2567169656471760211)
XLA Ops:
  0.0 108.9 %denoise.1 = bf16[2048,256]{1,0:T(8,128)(2,1)} custom-call(s32[128]{0:T(128)} %count_ref.1, s32[2,192]{1,0:T(2,128)} %bitcast.5, bf16[2048,256]{1,0:T(8,128)(2,1)} %bitcast.4), custom_call_target="tpu_custom_call" | custom-call | tf_op jit(solution)/shard_map/denoise/pallas_call | solution.py:474
  108.9 2.3 %copy.5 = bf16[16,128,256]{2,1,0:T(8,128)(2,1)} copy(bf16[16,128,256]{2,1,0:T(8,128)(2,1)} %bitcast.3) | data formatting | bytes 2097152

commit v6 on v5

--- a/solution.py
+++ b/solution.py
@@ -184,16 +184,12 @@
         def _():
             act(moved(turn, 4, RIGHT, SIDE_A, HALF + order, down))
 
+    def over_copy(turn, piece):
+        return moved(turn, 5, ACROSS, jnp.where(edge, SIDE_B, SIDE_A), piece, over)
+
     def over_copies(turn, order, act):
         for piece in (order, HALF + order):
-
-            @pl.when(edge)
-            def _():
-                act(moved(turn, 5, ACROSS, SIDE_B, piece, over))
-
-            @pl.when(jnp.logical_not(edge))
-            def _():
-                act(moved(turn, 5, ACROSS, SIDE_A, piece, over))
+            act(over_copy(turn, piece))
 
     def onward_copies(turn, order, act):
         at_first, at_last = passing(order)
@@ -240,9 +236,9 @@
         @pl.when((at > 0) & (place >= BATCH))
         def _():
             send_rest(turn, order + BATCH)
-            arrived(turn, ACROSS, order)
-            arrived(turn, ACROSS, HALF + order)
-            over_copies(turn, order, start)
+            for piece in (order, HALF + order):
+                arrived(turn, ACROSS, piece)
+                over_copy(turn, piece).start()
 
         @pl.when(at == PIECES)
         def _():

time: 111 us -> 111 us (level)
  no operation moved by 1% of the time
where the time goes in v6:
time: 111 us
  Pallas kernels  109 us (98%)
  local copies, waits for them, and re-layouts  2.29 us (2%)
    pallas_call x1, Pallas kernels, on_device(): pl.pallas_call(functools.partial(kernel, shape, (leaves, points)), out_sh...  109 us
    unnamed x1, local copies, waits for them, and re-layouts  2.29 us

profile of v6, /device:TPU:1, one launch (start us, length us, event | category | flops | bytes accessed | tf_op | source)
XLA Modules:
  0.0 111.2 jit_solution(5273092987997633848)
XLA Ops:
  0.0 108.9 %denoise.1 = bf16[2048,256]{1,0:T(8,128)(2,1)} custom-call(s32[128]{0:T(128)} %count_ref.1, s32[2,192]{1,0:T(2,128)} %bitcast.5, bf16[2048,256]{1,0:T(8,128)(2,1)} %bitcast.4), custom_call_target="tpu_custom_call" | custom-call | tf_op jit(solution)/shard_map/denoise/pallas_call | solution.py:470
  108.9 2.3 %copy.5 = bf16[16,128,256]{2,1,0:T(8,128)(2,1)} copy(bf16[16,128,256]{2,1,0:T(8,128)(2,1)} %bitcast.3) | data formatting | bytes 2097152
